TPU v7x, 32 devices: a whole 2x2x4 slice. The times are simulated.
32 devices in a mesh: group: 2 (over core), fsdp: 4 (over y, x), ep: 4 (over z).
Axes of the slice: x: 2, y: 2, z: 4, core: 2. Of those that a mesh axis runs over, the one named last changes fastest.
Arguments:
- batch: bfloat16 [2, 4, 512, 1536], P('group', None, 'fsdp'), may hold values from -6 to 6
- expert_ids: int32 [2, 4, 512, 4], P('group', None, 'fsdp'), may hold values from 0 to 7, all different within a row; in each aligned block of 128 rows (0 to 127, 128 to 255, ..., all dimensions but the last counted through in order) at most 96 rows name the same one
- route_weights: float32 [2, 4, 512, 4], P('group', None, 'fsdp'), may hold values from 0.1 to 1
- weights: bfloat16 [4, 3, 1536, 1536], P('ep', None, 'fsdp'), may hold values from -0.15625 to 0.15625
- cotangent: bfloat16 [4, 512, 1536], P(None, 'fsdp'), may hold values from -6 to 6
- master: float32 [4, 3, 1536, 1536], P('ep', None, 'fsdp', 'group'), may hold values from -0.15625 to 0.15625
- moment_one: float32 [4, 3, 1536, 1536], P('ep', None, 'fsdp', 'group'), may hold values from -0.013258252 to 0.013258252
- moment_two: float32 [4, 3, 1536, 1536], P('ep', None, 'fsdp', 'group'), may hold values from 8.789063e-09 to 1.7578125e-07
Outputs:
- layer_out: bfloat16 [2, 4, 512, 1536], P('group', None, ('fsdp', 'ep'))
- master_next: float32 [4, 3, 1536, 1536], P('ep', None, 'fsdp', 'group')
- moment_one_next: float32 [4, 3, 1536, 1536], P('ep', None, 'fsdp', 'group')
- moment_two_next: float32 [4, 3, 1536, 1536], P('ep', None, 'fsdp', 'group')
- serving: bfloat16 [4, 3, 1536, 1536], P('ep', None, 'fsdp')
Inputs may be any that keep to these rules, and one draw needn't show every extreme that they name: `expert_ids`: the 4 ids of a row differ. In each aligned block of 128 rows (one step of one fsdp index in one slot) no expert is named more than 96 times, a bound that some block reaches.
All inputs are finite; a program needn't handle non-finite values.
Results may differ from a plain program's by a relative error of at most 0.019.
Values may be sent and summed in bfloat16 or wider, within the bound.
A program may use at most 192 MiB of HBM per device.

v0:
```python
import jax
import jax.numpy as jnp
from jax import lax
from jax.sharding import PartitionSpec as P

CAP = 96


GLU_ALPHA = 1.702
BETA_ONE = 0.9
BETA_TWO = 0.999
LEARN_RATE = 0.01
ADAM_EPS = 1e-08
BIAS_ONE = 1.0 - 0.9**10
BIAS_TWO = 1.0 - 0.999**10


def shifted(value, axis, steps):
    count = lax.axis_size(axis)
    leading, last = (max(0, -steps), min(count, count - steps))
    return lax.ppermute(value, axis, [(source, source + steps) for source in range(leading, last)])


def contract_rows(left, right):
    return lax.dot_general(
        left, right, (((0,), (0,)), ((), ())), preferred_element_type=jnp.float32
    )


def local(batch, expert_ids, route_weights, weights, cotangent, master, moment_one, moment_two):
    rows_x = batch[0]
    route_ids = expert_ids[0]
    route_probs = route_weights[0]
    step_count, row_count, feat_count = rows_x.shape
    hidden_count = weights.shape[3]
    half_cols = hidden_count // 2
    expert = lax.axis_index("ep")
    core_index = lax.axis_index("group")
    is_learner = core_index == 0
    gathered = lax.all_gather(weights, "fsdp", axis=2, tiled=True)
    w_gate = gathered[0, 0]
    w_up = gathered[0, 1]
    w_down = gathered[0, 2]
    matches = route_ids == expert
    row_coef = jnp.sum(jnp.where(matches, route_probs, jnp.float32(0.0)), axis=2)
    routed = jnp.any(matches, axis=2)
    slot_index = jnp.cumsum(routed.astype(jnp.int32), axis=1) - 1
    slot_iota = lax.broadcasted_iota(jnp.int32, (step_count, CAP, row_count), 1)
    onehot = routed[:, None, :] & (slot_index[:, None, :] == slot_iota)
    picker = onehot.astype(jnp.bfloat16)
    slot_rows = jnp.einsum("scr,srd->scd", picker, rows_x, preferred_element_type=jnp.float32)
    slot_rows = slot_rows.astype(jnp.bfloat16).reshape(step_count * CAP, feat_count)
    slot_coef = jnp.einsum(
        "scr,sr->sc", onehot.astype(jnp.float32), row_coef, precision=lax.Precision.HIGHEST
    )
    gate_pre = jnp.dot(slot_rows, w_gate, preferred_element_type=jnp.float32)
    up_pre = jnp.dot(slot_rows, w_up, preferred_element_type=jnp.float32)
    sig_gate = jax.nn.sigmoid(GLU_ALPHA * gate_pre)
    activated = gate_pre * sig_gate
    hidden = (activated * (up_pre + 1.0)).astype(jnp.bfloat16)
    projected = lax.dot_general(
        hidden, w_down, (((1,), (1,)), ((), ())), preferred_element_type=jnp.float32
    )
    slot_terms = (slot_coef.reshape(-1)[:, None] * projected).astype(jnp.bfloat16)
    slot_terms = slot_terms.reshape(step_count, CAP, feat_count)
    row_terms = jnp.einsum("scr,scd->srd", picker, slot_terms, preferred_element_type=jnp.float32)
    mixed = lax.psum_scatter(row_terms.astype(jnp.bfloat16), "ep", scatter_dimension=1, tiled=True)
    layer_out = mixed[None]
    tokens_total = step_count * row_count * lax.axis_size("fsdp")

    def learner_side(unused):
        dy_slots = jnp.einsum("scr,srd->scd", picker, cotangent, preferred_element_type=jnp.float32)
        dy_scaled = (
            (slot_coef[:, :, None] * dy_slots)
            .astype(jnp.bfloat16)
            .reshape(step_count * CAP, feat_count)
        )
        grad_down = contract_rows(dy_scaled, hidden)
        grad_hidden = jnp.dot(dy_scaled, w_down, preferred_element_type=jnp.float32)
        gate_slope = sig_gate + GLU_ALPHA * gate_pre * sig_gate * (1.0 - sig_gate)
        d_up = (grad_hidden * activated).astype(jnp.bfloat16)
        d_gate = (grad_hidden * (up_pre + 1.0) * gate_slope).astype(jnp.bfloat16)
        grad_gate = contract_rows(slot_rows, d_gate)
        grad_up = contract_rows(slot_rows, d_up)
        return jnp.stack([grad_gate, grad_up, grad_down])[None] / tokens_total

    def rollout_side(unused):
        return jnp.zeros((1, 3, feat_count, hidden_count), jnp.float32)

    grads = lax.cond(is_learner, learner_side, rollout_side, 0)
    crossed = shifted(grads[..., half_cols:].astype(jnp.bfloat16), "group", 1)
    own_terms = jnp.where(is_learner, grads[..., :half_cols].astype(jnp.bfloat16), crossed)
    grad_own = lax.psum_scatter(
        own_terms.astype(jnp.float32).astype(jnp.bfloat16), "fsdp", scatter_dimension=2, tiled=True
    ).astype(jnp.float32)
    moment_one_next = BETA_ONE * moment_one + (1.0 - BETA_ONE) * grad_own
    moment_two_next = BETA_TWO * moment_two + (1.0 - BETA_TWO) * grad_own * grad_own
    master_next = master - LEARN_RATE * (moment_one_next / BIAS_ONE) / (
        jnp.sqrt(moment_two_next / BIAS_TWO) + ADAM_EPS
    )
    serving = lax.all_gather(master_next.astype(jnp.bfloat16), "group", axis=3, tiled=True)
    return (layer_out, master_next, moment_one_next, moment_two_next, serving)


def solution(mesh):
    return jax.shard_map(
        local,
        mesh=mesh,
        in_specs=(
            P("group", None, "fsdp", None),
            P("group", None, "fsdp", None),
            P("group", None, "fsdp", None),
            P("ep", None, "fsdp", None),
            P(None, "fsdp", None),
            P("ep", None, "fsdp", "group"),
            P("ep", None, "fsdp", "group"),
            P("ep", None, "fsdp", "group"),
        ),
        out_specs=(
            P("group", None, ("fsdp", "ep"), None),
            P("ep", None, "fsdp", "group"),
            P("ep", None, "fsdp", "group"),
            P("ep", None, "fsdp", "group"),
            P("ep", None, "fsdp", None),
        ),
        check_vma=False,
    )
```

profile of v0, /device:TPU:0, one launch (start us, length us, event | category | flops | bytes accessed | tf_op | source)
XLA Modules:
  0.0 380.3 jit_solution(297925247871065021)
XLA Ops:
  7.2 0.7 all-gather.3.cloned.1.call-update
  9.2 139.0 %all-gather.3.cloned.1.call-done = bf16[1,3,1536,1536]{3,2,1,0:T(8,128)(2,1)} async-done(((bf16[1,3,384,1536]{3,2,1,0:T(8,128)(2,1)}), bf16[1,3,1536,1536]{3,2,1,0:T(8,128)(2,1)}) %all-gather.3.cloned.1.call-update) | async-done | bytes 14155792 | tf_op jit(solution)/shard_map/all_gather | solution.py:40
  148.2 4.8 %slice_bitcast_fusion = bf16[1536,1536]{1,0:T(8,128)(2,1)} fusion(bf16[1,3,1536,1536]{3,2,1,0:T(8,128)(2,1)} %all-gather.3.cloned.1.call-done), kind=kLoop, calls=%fused_computation.14 | loop fusion | bytes 9437184 | tf_op jit(solution)/shard_map/squeeze | solution.py:43
  153.0 4.3 %fusion.6 = f32[384,1536]{1,0:T(8,128)S(1)} fusion(bf16[384,1536]{1,0:T(8,128)(2,1)S(1)} %bitcast.45, bf16[1,3,1536,1536]{3,2,1,0:T(8,128)(2,1)} %all-gather.3.cloned.1.call-done), kind=kOutput, calls=%fused_computation.18 | convolution fusion | flops 1811939328 | bytes 8257536 | tf_op jit(solution)/shard_map/dot_general | solution.py:56
  157.3 8.7 %multiply_convert_fusion.4 = (bf16[384,1536]{1,0:T(8,128)(2,1)}, f32[384,1536]{1,0:T(8,128)}, f32[384,1536]{1,0:T(8,128)}, f32[384,1536]{1,0:T(8,128)}) fusion(f32[384,1536]{1,0:T(8,128)S(1)} %fusion.6, bf16[384,1536]{1,0:T(8,128)(2,1)S(1)} %bitcast.46, bf16[1,3,1536,1536]{3,2,1,0:T(8,128)(2,1)} %all-gather.3.cloned.1.call-done), kind=kOutput, calls=%fused_computation.27 | convolution fusion | flops 1816657920 | bytes 16515072 | tf_op jit(solution)/shard_map/dot_general | solution.py:57
  166.0 22.8 %conditional.1 = (bf16[1,3,1536,1536]{2,3,1,0:T(8,128)(2,1)}) conditional(s32[]{:T(128)} %convert_element_type.50, () %tuple.14, (f32[4,96]{1,0:T(4,128)S(1)}, bf16[4,96,128]{2,1,0:T(8,128)(2,1)S(1)}, bf16[4,128,1536]{2,1,0:T(8,128)(2,1)}, bf16[1536,1536]{1,0:T(8,128)(2,1)}, f32[384,1536]{1,0:T(8,128)}, /*index=5*/f32[384,1536]{1,0:T(8,128)S(1)}, ...), branch_computations={%region_4.5_spmd, %region_5.6_spmd} | conditional | flops 7434731520 | bytes 138512000 | solution.py:90
  166.0 2.8 fusion
  168.8 2.7 convolution_bitcast_fusion
  171.6 2.0 fusion.30
  173.6 2.8 convolution_bitcast_fusion.1
  176.3 5.1 %convolution_bitcast_fusion.2 = f32[1,1,1536,1536]{2,3,1,0:T(8,128)S(1)} fusion(bf16[384,1536]{1,0:T(8,128)(2,1)S(1)} %get-tuple-element.30, f32[384,1536]{1,0:T(8,128)} %get-tuple-element.28, f32[384,1536]{1,0:T(8,128)} %copy-done.3, f32[384,1536]{1,0:T(8,128)S(1)} %fusion.30, f32[384,1536]{1,0:T(8,128)} %get-tuple-element.27), kind=kOutput, calls=%fused_computation.3 | convolution fusion | flops 1817247744 | bytes 20054016 | tf_op jit(solution)/shard_map/cond/branch_1_fun/dot_general | solution.py:25
  181.5 7.3 %maximum_multiply_fusion = bf16[1,3,1536,1536]{2,3,1,0:T(8,128)(2,1)} fusion(f32[1,1,1536,1536]{2,3,1,0:T(8,128)S(1)} %convolution_bitcast_fusion, f32[1,1,1536,1536]{2,3,1,0:T(8,128)S(1)} %convolution_bitcast_fusion.1, f32[1,1,1536,1536]{2,3,1,0:T(8,128)S(1)} %convolution_bitcast_fusion.2), kind=kLoop, calls=%fused_computation | loop fusion | flops 28311552 | bytes 42467328 | tf_op jit(solution)/shard_map/cond/branch_1_fun/div | solution.py:85
  188.8 18.7 %copy.15 = bf16[1,3,1536,1536]{3,2,1,0:T(8,128)(2,1)} copy(bf16[1,3,1536,1536]{2,3,1,0:T(8,128)(2,1)} %get-tuple-element.60) | data formatting | bytes 28311552 | tf_op jit(solution)/shard_map/cond | solution.py:90
  207.5 3.5 slice.26
  211.0 4.2 %collective-permute-start = (bf16[1,3,1536,768]{3,2,1,0:T(8,128)(2,1)S(1)}, bf16[1,3,1536,768]{3,2,1,0:T(8,128)(2,1)}, u32[]{:S(2)}, u32[]{:S(2)}) collective-permute-start(bf16[1,3,1536,768]{3,2,1,0:T(8,128)(2,1)S(1)} %slice.26), channel_id=1, source_target_pairs={{0,16},{1,17},{2,18},{3,19},{4,20},{5,21},{6,22},{7,23},{8,24},{9,... | collective-permute-start | bytes 21233672 | tf_op jit(solution)/shard_map/ppermute | solution.py:21
  215.2 8.2 %collective-permute-done = bf16[1,3,1536,768]{3,2,1,0:T(8,128)(2,1)} collective-permute-done((bf16[1,3,1536,768]{3,2,1,0:T(8,128)(2,1)S(1)}, bf16[1,3,1536,768]{3,2,1,0:T(8,128)(2,1)}, u32[]{:S(2)}, u32[]{:S(2)}) %collective-permute-start) | collective-permute-done | bytes 7077920 | tf_op jit(solution)/shard_map/ppermute | solution.py:21
  223.3 6.6 %slice_select_fusion = bf16[1,3,1536,768]{3,2,1,0:T(8,128)(2,1)} fusion(bf16[1,3,1536,768]{3,2,1,0:T(8,128)(2,1)} %collective-permute-done, bf16[1,3,1536,1536]{3,2,1,0:T(8,128)(2,1)} %copy.15, pred[]{:T(512)S(6)} %eq.22), kind=kLoop, calls=%fused_computation.12 | loop fusion | flops 3538944 | bytes 21233664 | tf_op jit(solution)/shard_map/jit(_where)/select_n | solution.py:92
  230.0 78.9 %reduce-scatter.5.cloned.1.call-done = bf16[1,3,384,768]{3,2,1,0:T(8,128)(2,1)} async-done(((bf16[1,3,1536,768]{3,2,1,0:T(8,128)(2,1)}), bf16[1,3,384,768]{3,2,1,0:T(8,128)(2,1)}) %reduce-scatter.5.cloned.1.call-update) | async-done | bytes 1769488 | tf_op jit(solution)/shard_map/reduce_scatter | solution.py:93
  308.9 8.6 %fusion.26 = (bf16[1,3,384,768]{3,2,1,0:T(8,128)(2,1)}, f32[1,3,384,768]{3,2,1,0:T(8,128)}, f32[1,3,384,768]{3,2,1,0:T(8,128)}, f32[1,3,384,768]{3,2,1,0:T(8,128)}) fusion(f32[1,3,384,768]{3,2,1,0:T(8,128)} %param.15, bf16[1,3,384,768]{3,2,1,0:T(8,128)(2,1)} %reduce-scatter.5.cloned.1.call-done, f32[1,3,384,768]{3,2,1,0:T(8,128)} %param.16, ...), kind=kLoop, calls=%fused_computation.45 | loop fusion | flops 12386304 | bytes 24772608 | tf_op jit(solution)/shard_map/convert_element_type | solution.py:101
  317.7 5.8 %fusion.9 = bf16[384,1536]{1,0:T(8,128)(2,1)S(1)} fusion(f32[384]{0:T(512)S(1)} %mul.78, f32[384,1536]{1,0:T(8,128)} %get-tuple-element.49, bf16[1,3,1536,1536]{3,2,1,0:T(8,128)(2,1)} %all-gather.3.cloned.1.call-done, f32[384,1536]{1,0:T(8,128)} %copy-done.2), kind=kOutput, calls=%fused_computation.25 | convolution fusion | flops 1817837568 | bytes 10618368 | tf_op jit(solution)/shard_map/dot_general | solution.py:61
  323.5 1.8 convolution_convert_fusion
  325.3 5.1 %all-gather.5.cloned.1.call-done = bf16[1,3,384,1536]{3,2,1,0:T(8,128)(2,1)} async-done(((bf16[1,3,384,768]{3,2,1,0:T(8,128)(2,1)}), bf16[1,3,384,1536]{3,2,1,0:T(8,128)(2,1)}) %all-gather.5.cloned.1.call-update) | async-done | bytes 3538960 | tf_op jit(solution)/shard_map/all_gather | solution.py:101
  330.4 39.2 %reduce-scatter.3.cloned.1.call-done = bf16[4,32,1536]{2,1,0:T(8,128)(2,1)} async-done(((bf16[4,128,1536]{2,1,0:T(8,128)(2,1)}), bf16[4,32,1536]{2,1,0:T(8,128)(2,1)}) %reduce-scatter.3.cloned.1.call-update) | async-done | bytes 393232 | tf_op jit(solution)/shard_map/reduce_scatter | solution.py:67
  369.6 4.1 %copy.22 = bf16[1,3,384,1536]{3,2,1,0:T(8,128)(2,1)} copy(bf16[1,3,384,1536]{3,2,1,0:T(8,128)(2,1)} %all-gather.5.cloned.1.call-done) | data formatting | bytes 7077888
  (37 shorter events, 1.5 us)
Async XLA Ops:
  7.2 1.5 copy-start
  7.2 0.8 copy-start.7
  7.2 1.2 copy-start.6
  7.2 141.0 %all-gather.3.cloned.1.call-start = ((), (), s32[]{:S(2)}) async-start(), calls=%async_computation.2 | async-start | bytes 17694720 | tf_op jit(solution)/shard_map/all_gather | solution.py:40
  7.9 301.0 %reduce-scatter.5.cloned.1.call-start = ((), (), s32[]{:S(2)}) async-start(), calls=%async_computation.4 | async-start | bytes 8847360 | tf_op jit(solution)/shard_map/reduce_scatter | solution.py:93
  157.3 8.7 %copy-start.2 = (f32[384,1536]{1,0:T(8,128)}, f32[384,1536]{1,0:T(8,128)S(1)}, u32[]{:S(2)}) copy-start(f32[384,1536]{1,0:T(8,128)S(1)} %fusion.6) | copy-start | bytes 7077892
  166.0 2.8 copy-start.3
  166.0 2.8 copy-start.5
  166.0 5.5 %slice-start = ((s8[4718592]{0:T(1024)(128)(4,1)}), s8[4194304]{0:T(1024)(128)(4,1)S(1)}, s32[]{:S(2)}) async-start(s8[4718592]{0:T(1024)(128)(4,1)} %bitcast.50), calls=%async_computation.6 | async-start | bytes 8388608 | tf_op jit(solution)/shard_map/cond
  168.8 2.7 slice-start.1
  171.6 2.0 copy-start.4
  211.0 12.3 %collective-permute-start = (bf16[1,3,1536,768]{3,2,1,0:T(8,128)(2,1)S(1)}, bf16[1,3,1536,768]{3,2,1,0:T(8,128)(2,1)}, u32[]{:S(2)}, u32[]{:S(2)}) collective-permute-start(bf16[1,3,1536,768]{3,2,1,0:T(8,128)(2,1)S(1)} %slice.26), channel_id=1, source_target_pairs={{0,16},{1,17},{2,18},{3,19},{4,20},{5,21},{6,22},{7,23},{8,24},{9,... | collective-permute-start | bytes 21233672 | tf_op jit(solution)/shard_map/ppermute | solution.py:21
  230.0 100.4 %all-gather.5.cloned.1.call-start = ((), (), s32[]{:S(2)}) async-start(), calls=%async_computation.5 | async-start | bytes 5308416 | tf_op jit(solution)/shard_map/all_gather | solution.py:101
  317.5 52.1 %reduce-scatter.3.cloned.1.call-start = ((), (), s32[]{:S(2)}) async-start(), calls=%async_computation.3 | async-start | bytes 1966080 | tf_op jit(solution)/shard_map/reduce_scatter | solution.py:67
  369.6 4.1 %copy-start.1 = (bf16[1,4,128,1536]{3,2,1,0:T(8,128)(2,1)S(1)}, bf16[1,4,128,1536]{3,2,1,0:T(8,128)(2,1)}, u32[]{:S(2)}) copy-start(bf16[1,4,128,1536]{3,2,1,0:T(8,128)(2,1)} %param.10) | copy-start | bytes 4718596
Sparse Core Ops, SparseCore 0:
  9.9 138.2 all-gather.2
  230.1 78.7 reduce-scatter.4
  317.7 12.6 all-gather.4
  333.1 36.4 reduce-scatter.2
where the time goes:
time: 381 us; the launch traced here: 380 us
  waiting for transfers between devices  271 us (71%)
  matrix products  36.6 us (10%)
  local copies, waits for them, and re-layouts  31.3 us (8%)
  other arithmetic  22.9 us (6%)
  between operations  13.9 us (4%)
  starting transfers between devices  4.32 us (1%)
    all_gather x1, waiting for transfers between devices, local(): gathered = lax.all_gather(weights, 'fsdp', axis=2, tiled=True)  139 us
    reduce_scatter x1, waiting for transfers between devices, local(): lax.psum_scatter(own_terms.astype(jnp.float32).astype(jnp.bfloat16), 'fsd...  78.9 us
    reduce_scatter x1, waiting for transfers between devices, local(): lax.psum_scatter(row_terms.astype(jnp.bfloat16), 'ep', scatter_dimension=...  39.2 us
    cond x1, local copies, waits for them, and re-layouts, local(): grads = lax.cond(is_learner, learner_side, rollout_side, 0)  18.7 us
    dot_general x3, matrix products, contract_rows(): lax.dot_general(left, right, (((0,), (0,)), ((), ())), preferred_element_...  10.6 us
    dot_general x1, matrix products, local(): up_pre = jnp.dot(slot_rows, w_up, preferred_element_type=jnp.float32)  8.68 us
    convert_element_type x1, other arithmetic, local(): master_next.astype(jnp.bfloat16)  8.58 us
    ppermute x1, waiting for transfers between devices, shifted(): lax.ppermute(value, axis, [(source, source + steps) for source in range(l...  8.16 us
  transfers between devices with their start and end apart: 5, of which 5 were waited for; matrix products, arithmetic and copies ran while one was open for 2% of the time, Pallas kernels for 0%

commit v1 on v0

--- a/solution.py
+++ b/solution.py
@@ -1,11 +1,14 @@
+import functools
+
 import jax
 import jax.numpy as jnp
 from jax import lax
+from jax.experimental import pallas as pl
+from jax.experimental.pallas import tpu as pltpu
 from jax.sharding import PartitionSpec as P
 
 CAP = 96
-
-
+MESH = pl.DeviceIdType.MESH
 GLU_ALPHA = 1.702
 BETA_ONE = 0.9
 BETA_TWO = 0.999
@@ -25,6 +28,368 @@
     return lax.dot_general(
         left, right, (((0,), (0,)), ((), ())), preferred_element_type=jnp.float32
     )
+
+
+def adam(grad_own, master, moment_one, moment_two):
+    moment_one_next = BETA_ONE * moment_one + (1.0 - BETA_ONE) * grad_own
+    moment_two_next = BETA_TWO * moment_two + (1.0 - BETA_TWO) * grad_own * grad_own
+    master_next = master - LEARN_RATE * (moment_one_next / BIAS_ONE) / (
+        jnp.sqrt(moment_two_next / BIAS_TWO) + ADAM_EPS
+    )
+    return master_next, moment_one_next, moment_two_next
+
+
+def layer_kernel(
+    ep_count, tokens_total, ids, probs, x, ct, w, lo_out, grad_out,
+    wts, gate, up, gh, onehots, coefs, xs, dys, gx, gdy, hid, gb, gs, sg,
+    r1x, r1y, px, py, rt, rr,
+    own_sem, dsx, drx, dsy, dry, fsx, frx, fsy, fry, psend, precv,
+    lsend, lrecv, r1s, r1r, pps, ppr, es, er,
+):
+    g, f, e = lax.axis_index("group"), lax.axis_index("fsdp"), lax.axis_index("ep")
+    fx, fy = f % 2, f // 2
+    xn, yn, dn, pg = fy * 2 + 1 - fx, (1 - fy) * 2 + fx, 3 - f, 1 - g
+    steps, row_count, feat = x.shape
+    dep = w.shape[1]
+    half_rows, quarter = dep // 2, dep // 4
+    hidden_count = w.shape[2]
+    half_cols = hidden_count // 2
+    slots = steps * CAP
+    x_id, y_id, p_id = (g, xn, e), (g, yn, e), (pg, f, e)
+    order = (2, 0, 1)
+
+    barrier = pltpu.get_barrier_semaphore()
+    peers = [(g, f, (e + k) % ep_count) for k in range(1, ep_count)]
+    greet = [x_id, y_id, p_id] + peers
+    for peer in greet:
+        pl.semaphore_signal(barrier, inc=1, device_id=peer, device_id_type=MESH)
+    pl.semaphore_wait(barrier, len(greet))
+
+    def remote(src, dst, send, recv, target):
+        return pltpu.make_async_remote_copy(
+            src_ref=src, dst_ref=dst, send_sem=send, recv_sem=recv,
+            device_id=target, device_id_type=MESH,
+        )
+
+    base = pl.multiple_of(g * half_rows, half_rows)
+    mine = pl.ds(base, half_rows)
+    first = pl.ds(base, quarter)
+    second = pl.ds(pl.multiple_of(base + quarter, quarter), quarter)
+
+    def direct(m):
+        return (
+            remote(w.at[m, mine], wts.at[m, f, mine], dsx.at[m], drx.at[m], x_id),
+            remote(w.at[m, mine], wts.at[m, f, mine], dsy.at[m], dry.at[m], y_id),
+        )
+
+    def relays(m):
+        return (
+            remote(wts.at[m, xn, first], wts.at[m, xn, first], fsy.at[m], fry.at[m], y_id),
+            remote(wts.at[m, yn, second], wts.at[m, yn, second], fsx.at[m], frx.at[m], x_id),
+        )
+
+    def share(m, place, source):
+        block = wts.at[m, source, mine]
+        return remote(block, block, psend.at[m, place], precv.at[m, place], p_id)
+
+    directs = {m: direct(m) for m in order}
+    forwards = {m: relays(m) for m in order}
+    shares = {m: [share(m, i, s) for i, s in enumerate((xn, yn, dn))] for m in order}
+
+    for m in order[:2]:
+        for copy in directs[m]:
+            copy.start()
+    owns = [pltpu.make_async_copy(w.at[m], wts.at[m, f], own_sem.at[m]) for m in range(3)]
+    for copy in owns:
+        copy.start()
+
+    match = ids[...] == e
+    row_coef = jnp.sum(jnp.where(match, probs[...], 0.0), axis=0)
+    routed = jnp.max(jnp.where(match, 1.0, 0.0), axis=0)
+    before = (
+        lax.broadcasted_iota(jnp.int32, (row_count, row_count), 0)
+        < lax.broadcasted_iota(jnp.int32, (row_count, row_count), 1)
+    )
+    rank = jnp.dot(
+        routed.astype(jnp.bfloat16),
+        jnp.where(before, 1.0, 0.0).astype(jnp.bfloat16),
+        preferred_element_type=jnp.float32,
+    ).astype(jnp.int32)
+    slot_iota = lax.broadcasted_iota(jnp.int32, (CAP, row_count), 0)
+    for s in range(steps):
+        hit = jnp.where(slot_iota == rank[s : s + 1, :], routed[s : s + 1, :], 0.0)
+        onehots[s] = hit.astype(jnp.bfloat16)
+        coef = jnp.sum(hit * row_coef[s : s + 1, :], axis=1, keepdims=True)
+        coefs[pl.ds(s * CAP, CAP), :] = jnp.broadcast_to(coef, (CAP, 128))
+
+    @pl.loop(0, steps)
+    def _(s):
+        place = pl.ds(pl.multiple_of(s * CAP, CAP), CAP)
+        picker = onehots[s]
+        coef = coefs[place, :][:, 0:1]
+        for c in range(4):
+            cols = pl.ds(c * dep, dep)
+            picked = jnp.dot(picker, x[s, :, cols], preferred_element_type=jnp.float32)
+            xs[c, place, :] = picked.astype(jnp.bfloat16)
+            picked = jnp.dot(picker, ct[s, :, cols], preferred_element_type=jnp.float32)
+            dys[c, place, :] = (coef * picked).astype(jnp.bfloat16)
+
+    to_rollout = [
+        remote(xs, gx, lsend.at[0], lrecv.at[0], p_id),
+        remote(dys, gdy, lsend.at[1], lrecv.at[1], p_id),
+    ] + [
+        remote(gs.at[i], gb.at[i], lsend.at[2 + i], lrecv.at[2 + i], p_id) for i in range(3)
+    ]
+
+    @pl.when(g == 0)
+    def _():
+        to_rollout[0].start()
+        to_rollout[1].start()
+        gx[...] = xs[...]
+        gdy[...] = dys[...]
+
+    tile = 512
+
+    def accumulate(m, source, start=False):
+        total, left = ((gate, xs), (up, xs), (gh, dys))[m]
+
+        @pl.loop(0, hidden_count // tile)
+        def _(n):
+            cols = pl.ds(pl.multiple_of(n * tile, tile), tile)
+            part = jnp.dot(left[source], wts[m, source, :, cols], preferred_element_type=jnp.float32)
+            total[:, cols] = part if start else total[:, cols] + part
+
+    for m in order:
+        owns[m].wait()
+        accumulate(m, f, True)
+
+    def take_direct(m, later):
+        to_x, to_y = directs[m]
+        relay_y, relay_x = forwards[m]
+        to_x.wait_recv()
+        relay_y.start()
+        shares[m][0].start()
+        to_y.wait_recv()
+        relay_x.start()
+        shares[m][1].start()
+        if later is not None:
+            for copy in directs[later]:
+                copy.start()
+        shares[m][0].wait_recv()
+        accumulate(m, xn)
+        shares[m][1].wait_recv()
+        accumulate(m, yn)
+
+    def take_diagonal(m):
+        relay_y, relay_x = forwards[m]
+        relay_y.wait_recv()
+        relay_x.wait_recv()
+        shares[m][2].start()
+        shares[m][2].wait_recv()
+        accumulate(m, dn)
+
+    take_direct(order[0], order[2])
+    take_direct(order[1], None)
+    take_diagonal(order[0])
+    take_direct(order[2], None)
+    take_diagonal(order[1])
+    take_diagonal(order[2])
+
+    block = 16
+
+    @pl.loop(0, slots // block)
+    def _(b):
+        rows = pl.ds(pl.multiple_of(b * block, block), block)
+        for side in range(2):
+            cols = pl.ds(side * half_cols, half_cols)
+            gate_pre, up_one = gate[rows, cols], up[rows, cols] + 1.0
+            back = gh[rows, cols]
+            sig = 1.0 / (1.0 + jnp.exp(-GLU_ALPHA * gate_pre))
+            act = gate_pre * sig
+            value = (act * up_one).astype(jnp.bfloat16)
+            slope = sig + GLU_ALPHA * act * (1.0 - sig)
+            d_up = (back * act).astype(jnp.bfloat16)
+            d_gate = (back * up_one * slope).astype(jnp.bfloat16)
+            hid[rows, cols] = value
+
+            @pl.when(g == 0)
+            def _():
+                keep = gb if side == 0 else gs
+                keep[0, rows, :] = d_gate
+                keep[1, rows, :] = d_up
+                keep[2, rows, :] = value
+
+    @pl.when(g == 0)
+    def _():
+        for copy in to_rollout[2:]:
+            copy.start()
+
+    @pl.when(g == 1)
+    def _():
+        for copy in to_rollout:
+            copy.wait_recv()
+
+    upper, lower = pl.ds(0, half_rows), pl.ds(half_rows, half_rows)
+
+    def gradient(m, owner):
+        left = gdy if m == 2 else gx
+        part = lax.dot_general(
+            left[owner], gb[m], (((0,), (0,)), ((), ())), preferred_element_type=jnp.float32
+        )
+        sg[m, owner] = (part * (1.0 / tokens_total)).astype(jnp.bfloat16)
+
+    firsts = {
+        m: (
+            remote(sg.at[m, dn, upper], r1x.at[m], r1s.at[m, 0], r1r.at[m, 0], x_id),
+            remote(sg.at[m, dn, lower], r1y.at[m], r1s.at[m, 1], r1r.at[m, 1], y_id),
+        )
+        for m in range(3)
+    }
+
+    def to_owner(m, i):
+        owner, target, land = ((xn, x_id, px), (yn, y_id, py))[i // 2]
+        rows = (upper, lower)[i % 2]
+        return remote(
+            sg.at[m, owner, rows], land.at[m, rows], pps.at[m, i], ppr.at[m, i], target
+        )
+
+    lasts = {m: [to_owner(m, i) for i in range(4)] for m in range(3)}
+
+    for m in range(3):
+        gradient(m, dn)
+        for copy in firsts[m]:
+            copy.start()
+        gradient(m, xn)
+        lasts[m][0].start()
+        gradient(m, yn)
+        lasts[m][3].start()
+    for m in range(3):
+        firsts[m][1].wait_recv()
+        sg[m, xn, lower, :] = (
+            sg[m, xn, lower, :].astype(jnp.float32) + r1y[m].astype(jnp.float32)
+        ).astype(jnp.bfloat16)
+        lasts[m][1].start()
+        firsts[m][0].wait_recv()
+        sg[m, yn, upper, :] = (
+            sg[m, yn, upper, :].astype(jnp.float32) + r1x[m].astype(jnp.float32)
+        ).astype(jnp.bfloat16)
+        lasts[m][2].start()
+
+        if m == 0:
+            share_rows = row_count // ep_count
+
+            @pl.loop(0, 4)
+            def _(c):
+                cols = pl.ds(pl.multiple_of(c * dep, dep), dep)
+                projected = lax.dot_general(
+                    hid[...], wts[2, c], (((1,), (1,)), ((), ())),
+                    preferred_element_type=jnp.float32,
+                )
+                term = (coefs[:, 0:1] * projected).astype(jnp.bfloat16)
+                for s in range(steps):
+                    spread = lax.dot_general(
+                        onehots[s], term[s * CAP : (s + 1) * CAP, :],
+                        (((0,), (0,)), ((), ())), preferred_element_type=jnp.float32,
+                    ).astype(jnp.bfloat16)
+                    for q in range(ep_count):
+                        rt[q, s, :, cols] = spread[q * share_rows : (q + 1) * share_rows, :]
+
+            terms = [
+                remote(rt.at[peers[k][2]], rr.at[k], es.at[k], er.at[k], peers[k])
+                for k in range(ep_count - 1)
+            ]
+            for copy in terms:
+                copy.start()
+
+    for m in range(3):
+        gradient(m, f)
+    for k in range(ep_count - 1):
+        terms[k].wait_recv()
+    total = rt[e].astype(jnp.float32)
+    for k in range(ep_count - 1):
+        total = total + rr[k].astype(jnp.float32)
+    lo_out[...] = total.astype(jnp.bfloat16)
+
+    for m in range(3):
+        for copy in lasts[m]:
+            copy.wait_recv()
+        grad_out[m] = (
+            sg[m, f].astype(jnp.float32) + px[m].astype(jnp.float32) + py[m].astype(jnp.float32)
+        )
+
+    for m in order:
+        for copy in (*directs[m], *forwards[m], *shares[m], *firsts[m], *lasts[m]):
+            copy.wait_send()
+    for copy in terms:
+        copy.wait_send()
+
+    @pl.when(g == 0)
+    def _():
+        for copy in to_rollout:
+            copy.wait_send()
+
+
+def kernel_local(
+    batch, expert_ids, route_weights, weights, cotangent, master, moment_one, moment_two
+):
+    steps, row_count, feat = batch.shape[1:]
+    top = expert_ids.shape[3]
+    dep, hidden_count = weights.shape[2:]
+    half = hidden_count // 2
+    slots = steps * CAP
+    ep_count = lax.axis_size("ep")
+    parts = lax.axis_size("fsdp")
+    tokens_total = steps * row_count * parts
+    ids = jnp.transpose(expert_ids[0], (2, 0, 1))
+    probs = jnp.transpose(route_weights[0], (2, 0, 1))
+    vmem = pl.BlockSpec(memory_space=pltpu.VMEM)
+    half_b, f32 = jnp.bfloat16, jnp.float32
+    dma = pltpu.SemaphoreType.DMA
+    layer_out, grad_own = pl.pallas_call(
+        functools.partial(layer_kernel, ep_count, tokens_total),
+        out_shape=(
+            jax.ShapeDtypeStruct((steps, row_count // ep_count, feat), half_b),
+            jax.ShapeDtypeStruct((3, dep, half), f32),
+        ),
+        in_specs=[vmem] * 4 + [pl.BlockSpec(memory_space=pl.ANY)],
+        out_specs=(vmem, vmem),
+        scratch_shapes=[
+            pltpu.VMEM((3, parts, dep, hidden_count), half_b),
+            pltpu.VMEM((slots, hidden_count), f32),
+            pltpu.VMEM((slots, hidden_count), f32),
+            pltpu.VMEM((slots, hidden_count), f32),
+            pltpu.VMEM((steps, CAP, row_count), half_b),
+            pltpu.VMEM((slots, 128), f32),
+            pltpu.VMEM((parts, slots, dep), half_b),
+            pltpu.VMEM((parts, slots, dep), half_b),
+            pltpu.VMEM((parts, slots, dep), half_b),
+            pltpu.VMEM((parts, slots, dep), half_b),
+            pltpu.VMEM((slots, hidden_count), half_b),
+            pltpu.VMEM((3, slots, half), half_b),
+            pltpu.VMEM((3, slots, half), half_b),
+            pltpu.VMEM((3, parts, dep, half), half_b),
+            pltpu.VMEM((3, dep // 2, half), half_b),
+            pltpu.VMEM((3, dep // 2, half), half_b),
+            pltpu.VMEM((3, dep, half), half_b),
+            pltpu.VMEM((3, dep, half), half_b),
+            pltpu.VMEM((ep_count, steps, row_count // ep_count, feat), half_b),
+            pltpu.VMEM((ep_count - 1, steps, row_count // ep_count, feat), half_b),
+        ]
+        + [dma((3,))] * 9
+        + [dma((3, 3))] * 2
+        + [dma((5,))] * 2
+        + [dma((3, 2))] * 2
+        + [dma((3, 4))] * 2
+        + [dma((ep_count - 1,))] * 2,
+        compiler_params=pltpu.CompilerParams(
+            collective_id=0, has_side_effects=True, vmem_limit_bytes=62 * 1024 * 1024
+        ),
+    )(ids, probs, batch[0], cotangent, weights[0])
+    master_next, moment_one_next, moment_two_next = adam(
+        grad_own[None], master, moment_one, moment_two
+    )
+    serving = lax.all_gather(master_next.astype(jnp.bfloat16), "group", axis=3, tiled=True)
+    return (layer_out[None], master_next, moment_one_next, moment_two_next, serving)
 
 
 def local(batch, expert_ids, route_weights, weights, cotangent, master, moment_one, moment_two):
@@ -104,7 +469,7 @@
 
 def solution(mesh):
     return jax.shard_map(
-        local,
+        kernel_local if mesh.shape["fsdp"] == 4 else local,
         mesh=mesh,
         in_specs=(
             P("group", None, "fsdp", None),

time: 381 us -> 174 us (0.46)
  waiting for transfers between devices: 271 us -> 13.5 us
  Pallas kernels: 0 us -> 130 us
  matrix products: 36.6 us -> 0 us
  local copies, waits for them, and re-layouts: 31.3 us -> 7.36 us
  other arithmetic: 22.9 us -> 8.86 us
  starting transfers between devices: 4.32 us -> 0.04 us
    all_gather x2 -> x1, waiting for transfers between devices: 144 us -> 13.5 us  [kernel_local(): lax.all_gather(master_next.astype(jnp.bfloat16), 'group', axis=3, tiled=T...]
    pallas_call x0 -> x1, Pallas kernels: none -> 130 us  [kernel_local(): pl.pallas_call(functools.partial(layer_kernel, ep_count, tokens_total), o...]
    reduce_scatter x2 -> x0, waiting for transfers between devices: 118 us -> none  [the longest x1 78.9 us: local(): lax.psum_scatter(own_terms.astype(jnp.float32).astype(jnp.bfloat16), 'fsd...]
    dot_general x11 -> x0, matrix products: 36.6 us -> none  [the longest x3 10.6 us: contract_rows(): lax.dot_general(left, right, (((0,), (0,)), ((), ())), preferred_element_...]
    cond x11 -> x0, local copies, waits for them, and re-layouts: 18.8 us -> none  [the longest x1 18.7 us: local(): grads = lax.cond(is_learner, learner_side, rollout_side, 0)]
    ppermute x1 -> x0, waiting for transfers between devices: 8.16 us -> none  [shifted(): lax.ppermute(value, axis, [(source, source + steps) for source in range(l...]
    div x1 -> x0, other arithmetic: 7.31 us -> none  [learner_side(): return jnp.stack([grad_gate, grad_up, grad_down])[None] / tokens_total]
    select_n x1 -> x0, other arithmetic: 6.62 us -> none  [local(): jnp.where(is_learner, grads[..., :half_cols].astype(jnp.bfloat16), crossed)]
  transfers between devices with their start and end apart: 5 -> 1, of which waited for: 5 -> 1; matrix products, arithmetic and copies ran while one was open for 2% -> 0% of each run, Pallas kernels for 0% -> 0%
where the time goes in v1:
time: 174 us
  Pallas kernels  130 us (75%)
  between operations  14 us (8%)
  waiting for transfers between devices  13.5 us (8%)
  other arithmetic  8.86 us (5%)
  local copies, waits for them, and re-layouts  7.36 us (4%)
    pallas_call x1, Pallas kernels, kernel_local(): pl.pallas_call(functools.partial(layer_kernel, ep_count, tokens_total), o...  130 us
    all_gather x1, waiting for transfers between devices, kernel_local(): lax.all_gather(master_next.astype(jnp.bfloat16), 'group', axis=3, tiled=T...  13.5 us
    convert_element_type x1, other arithmetic, kernel_local(): master_next.astype(jnp.bfloat16)  8.86 us
    unnamed x6, local copies, waits for them, and re-layouts  7.36 us
  transfers between devices with their start and end apart: 1, of which 1 were waited for; matrix products, arithmetic and copies ran while one was open for 0% of the time, Pallas kernels for 0%

profile of v1, /device:TPU:0, one launch (start us, length us, event | category | flops | bytes accessed | tf_op | source)
XLA Modules:
  0.0 173.8 jit_solution(12985406638749354253)
XLA Ops:
  7.2 0.0 all-gather.2.cloned.1.call-start
  7.2 1.3 copy.18
  8.5 1.3 copy.17
  9.8 130.0 %shard_map.119 = (bf16[4,32,1536]{2,1,0:T(8,128)(2,1)}, f32[3,384,768]{2,1,0:T(8,128)}) custom-call(s32[4,4,128]{2,1,0:T(4,128)} %bitcast.24, f32[4,4,128]{2,1,0:T(4,128)} %bitcast.25, bf16[4,128,1536]{2,1,0:T(8,128)(2,1)} %bitcast.22, bf16[4,128,1536]{2,1,0:T(8,128)(2,1)} %ct.1, bf16[3,384,1536]{2,1,0:T(8,128)(2,1)} %bitcast.21), custom_call_target="tpu_custom_call" | custom-call | tf_op jit(solution)/shard_map/pallas_call | solution.py:348
  139.8 0.0 copy-start
  139.8 8.9 %fusion.2 = (bf16[1,3,384,768]{3,2,1,0:T(8,128)(2,1)}, f32[1,3,384,768]{3,2,1,0:T(8,128)}, f32[1,3,384,768]{3,2,1,0:T(8,128)}, f32[1,3,384,768]{3,2,1,0:T(8,128)}) fusion(f32[1,3,384,768]{3,2,1,0:T(8,128)} %param.13, f32[3,384,768]{2,1,0:T(8,128)} %get-tuple-element.8, f32[1,3,384,768]{3,2,1,0:T(8,128)} %param.14, f32[1,3,384,768]{3,2,1,0:T(8,128)} %param.15), kind=kLoop, calls=%fused_computation.7 | loop fusion | flops 11501568 | bytes 26542080 | tf_op jit(solution)/shard_map/convert_element_type | solution.py:391
  148.7 0.0 all-gather.2.cloned.1.call-update
  148.7 13.5 %all-gather.2.cloned.1.call-done = bf16[1,3,384,1536]{3,2,1,0:T(8,128)(2,1)} async-done(((bf16[1,3,384,768]{3,2,1,0:T(8,128)(2,1)}), bf16[1,3,384,1536]{3,2,1,0:T(8,128)(2,1)}) %all-gather.2.cloned.1.call-update) | async-done | bytes 3538960 | tf_op jit(solution)/shard_map/all_gather | solution.py:391
  162.2 0.0 copy-done
  162.2 0.7 copy.21
  162.9 4.0 %copy.22 = bf16[1,3,384,1536]{3,2,1,0:T(8,128)(2,1)} copy(bf16[1,3,384,1536]{3,2,1,0:T(8,128)(2,1)} %all-gather.2.cloned.1.call-done) | data formatting | bytes 7077888
Async XLA Ops:
  7.2 155.0 %all-gather.2.cloned.1.call-start = ((), (), s32[]{:S(2)}) async-start(), calls=%async_computation | async-start | bytes 5308416 | tf_op jit(solution)/shard_map/all_gather | solution.py:391
  139.8 22.4 %copy-start = (bf16[4,32,1536]{2,1,0:T(8,128)(2,1)S(1)}, bf16[4,32,1536]{2,1,0:T(8,128)(2,1)}, u32[]{:S(2)}) copy-start(bf16[4,32,1536]{2,1,0:T(8,128)(2,1)} %get-tuple-element.7) | copy-start | bytes 1179652
Sparse Core Ops, SparseCore 0:
  148.8 13.3 all-gather.1

commit v2 on v1

--- a/solution.py
+++ b/solution.py
@@ -40,11 +40,12 @@
 
 
 def layer_kernel(
-    ep_count, tokens_total, ids, probs, x, ct, w, lo_out, grad_out,
+    ep_count, tokens_total, ids, probs, x, ct, w, master, moment_one, moment_two,
+    lo_out, grad_out, other,
     wts, gate, up, gh, onehots, coefs, xs, dys, gx, gdy, hid, gb, gs, sg,
-    r1x, r1y, px, py, rt, rr,
+    r1x, r1y, px, py, rt, rr, sv,
     own_sem, dsx, drx, dsy, dry, fsx, frx, fsy, fry, psend, precv,
-    lsend, lrecv, r1s, r1r, pps, ppr, es, er,
+    lsend, lrecv, r1s, r1r, pps, ppr, es, er, loads, svs, svr,
 ):
     g, f, e = lax.axis_index("group"), lax.axis_index("fsdp"), lax.axis_index("ep")
     fx, fy = f % 2, f // 2
@@ -56,7 +57,8 @@
     half_cols = hidden_count // 2
     slots = steps * CAP
     x_id, y_id, p_id = (g, xn, e), (g, yn, e), (pg, f, e)
-    order = (2, 0, 1)
+    order = (0, 1, 2)
+    grad_order = (2, 0, 1)
 
     barrier = pltpu.get_barrier_semaphore()
     peers = [(g, f, (e + k) % ep_count) for k in range(1, ep_count)]
@@ -104,8 +106,8 @@
         copy.start()
 
     match = ids[...] == e
-    row_coef = jnp.sum(jnp.where(match, probs[...], 0.0), axis=0)
-    routed = jnp.max(jnp.where(match, 1.0, 0.0), axis=0)
+    row_coef = jnp.sum(jnp.where(match, probs[...], 0.0), axis=1)
+    routed = jnp.max(jnp.where(match, 1.0, 0.0), axis=1)
     before = (
         lax.broadcasted_iota(jnp.int32, (row_count, row_count), 0)
         < lax.broadcasted_iota(jnp.int32, (row_count, row_count), 1)
@@ -163,7 +165,7 @@
         owns[m].wait()
         accumulate(m, f, True)
 
-    def take_direct(m, later):
+    def pass_on(m, later=None):
         to_x, to_y = directs[m]
         relay_y, relay_x = forwards[m]
         to_x.wait_recv()
@@ -175,12 +177,14 @@
         if later is not None:
             for copy in directs[later]:
                 copy.start()
+
+    def add_direct(m):
         shares[m][0].wait_recv()
         accumulate(m, xn)
         shares[m][1].wait_recv()
         accumulate(m, yn)
 
-    def take_diagonal(m):
+    def add_diagonal(m):
         relay_y, relay_x = forwards[m]
         relay_y.wait_recv()
         relay_x.wait_recv()
@@ -188,47 +192,6 @@
         shares[m][2].wait_recv()
         accumulate(m, dn)
 
-    take_direct(order[0], order[2])
-    take_direct(order[1], None)
-    take_diagonal(order[0])
-    take_direct(order[2], None)
-    take_diagonal(order[1])
-    take_diagonal(order[2])
-
-    block = 16
-
-    @pl.loop(0, slots // block)
-    def _(b):
-        rows = pl.ds(pl.multiple_of(b * block, block), block)
-        for side in range(2):
-            cols = pl.ds(side * half_cols, half_cols)
-            gate_pre, up_one = gate[rows, cols], up[rows, cols] + 1.0
-            back = gh[rows, cols]
-            sig = 1.0 / (1.0 + jnp.exp(-GLU_ALPHA * gate_pre))
-            act = gate_pre * sig
-            value = (act * up_one).astype(jnp.bfloat16)
-            slope = sig + GLU_ALPHA * act * (1.0 - sig)
-            d_up = (back * act).astype(jnp.bfloat16)
-            d_gate = (back * up_one * slope).astype(jnp.bfloat16)
-            hid[rows, cols] = value
-
-            @pl.when(g == 0)
-            def _():
-                keep = gb if side == 0 else gs
-                keep[0, rows, :] = d_gate
-                keep[1, rows, :] = d_up
-                keep[2, rows, :] = value
-
-    @pl.when(g == 0)
-    def _():
-        for copy in to_rollout[2:]:
-            copy.start()
-
-    @pl.when(g == 1)
-    def _():
-        for copy in to_rollout:
-            copy.wait_recv()
-
     upper, lower = pl.ds(0, half_rows), pl.ds(half_rows, half_rows)
 
     def gradient(m, owner):
@@ -255,7 +218,7 @@
 
     lasts = {m: [to_owner(m, i) for i in range(4)] for m in range(3)}
 
-    for m in range(3):
+    def open_sum(m):
         gradient(m, dn)
         for copy in firsts[m]:
             copy.start()
@@ -263,7 +226,8 @@
         lasts[m][0].start()
         gradient(m, yn)
         lasts[m][3].start()
-    for m in range(3):
+
+    def relay_sum(m):
         firsts[m][1].wait_recv()
         sg[m, xn, lower, :] = (
             sg[m, xn, lower, :].astype(jnp.float32) + r1y[m].astype(jnp.float32)
@@ -275,47 +239,150 @@
         ).astype(jnp.bfloat16)
         lasts[m][2].start()
 
-        if m == 0:
-            share_rows = row_count // ep_count
-
-            @pl.loop(0, 4)
-            def _(c):
-                cols = pl.ds(pl.multiple_of(c * dep, dep), dep)
-                projected = lax.dot_general(
-                    hid[...], wts[2, c], (((1,), (1,)), ((), ())),
-                    preferred_element_type=jnp.float32,
-                )
-                term = (coefs[:, 0:1] * projected).astype(jnp.bfloat16)
-                for s in range(steps):
-                    spread = lax.dot_general(
-                        onehots[s], term[s * CAP : (s + 1) * CAP, :],
-                        (((0,), (0,)), ((), ())), preferred_element_type=jnp.float32,
-                    ).astype(jnp.bfloat16)
-                    for q in range(ep_count):
-                        rt[q, s, :, cols] = spread[q * share_rows : (q + 1) * share_rows, :]
-
-            terms = [
-                remote(rt.at[peers[k][2]], rr.at[k], es.at[k], er.at[k], peers[k])
-                for k in range(ep_count - 1)
-            ]
-            for copy in terms:
-                copy.start()
-
-    for m in range(3):
+    pass_on(0, 2)
+    add_direct(0)
+    pass_on(1)
+    add_direct(1)
+    add_diagonal(0)
+    pass_on(2)
+    add_diagonal(1)
+
+    block = 16
+
+    @pl.loop(0, slots // block)
+    def _(b):
+        rows = pl.ds(pl.multiple_of(b * block, block), block)
+        for side in range(2):
+            cols = pl.ds(side * half_cols, half_cols)
+            gate_pre = gate[rows, cols]
+            sig = 1.0 / (1.0 + jnp.exp(-GLU_ALPHA * gate_pre))
+            value = (gate_pre * sig * (up[rows, cols] + 1.0)).astype(jnp.bfloat16)
+            hid[rows, cols] = value
+
+            @pl.when(g == 0)
+            def _():
+                (gb if side == 0 else gs)[2, rows, :] = value
+
+    @pl.when(g == 0)
+    def _():
+        to_rollout[4].start()
+
+    @pl.when(g == 1)
+    def _():
+        for i in (0, 1, 4):
+            to_rollout[i].wait_recv()
+
+    open_sum(2)
+    add_direct(2)
+    add_diagonal(2)
+
+    @pl.when(g == 0)
+    def _():
+        @pl.loop(0, slots // block)
+        def _(b):
+            rows = pl.ds(pl.multiple_of(b * block, block), block)
+            for side in range(2):
+                cols = pl.ds(side * half_cols, half_cols)
+                gate_pre, up_one = gate[rows, cols], up[rows, cols] + 1.0
+                back = gh[rows, cols]
+                sig = 1.0 / (1.0 + jnp.exp(-GLU_ALPHA * gate_pre))
+                act = gate_pre * sig
+                slope = sig + GLU_ALPHA * act * (1.0 - sig)
+                keep = gb if side == 0 else gs
+                keep[0, rows, :] = (back * up_one * slope).astype(jnp.bfloat16)
+                keep[1, rows, :] = (back * act).astype(jnp.bfloat16)
+
+        to_rollout[2].start()
+        to_rollout[3].start()
+
+    def load(i):
+        spot = pl.ds((i % 2) * half_cols, half_cols)
+        return [
+            pltpu.make_async_copy(src.at[grad_order[i]], dst.at[:, spot], loads.at[i, k])
+            for k, (src, dst) in enumerate(((master, gate), (moment_one, up), (moment_two, gh)))
+        ]
+
+    for i in range(2):
+        for copy in load(i):
+            copy.start()
+
+    relay_sum(2)
+
+    @pl.when(g == 1)
+    def _():
+        for i in (2, 3):
+            to_rollout[i].wait_recv()
+
+    open_sum(0)
+    open_sum(1)
+
+    share_rows = row_count // ep_count
+
+    @pl.loop(0, 4)
+    def _(c):
+        cols = pl.ds(pl.multiple_of(c * dep, dep), dep)
+        projected = lax.dot_general(
+            hid[...], wts[2, c], (((1,), (1,)), ((), ())),
+            preferred_element_type=jnp.float32,
+        )
+        term = (coefs[:, 0:1] * projected).astype(jnp.bfloat16)
+        for s in range(steps):
+            spread = lax.dot_general(
+                onehots[s], term[s * CAP : (s + 1) * CAP, :],
+                (((0,), (0,)), ((), ())), preferred_element_type=jnp.float32,
+            ).astype(jnp.bfloat16)
+            for q in range(ep_count):
+                rt[q, s, :, cols] = spread[q * share_rows : (q + 1) * share_rows, :]
+
+    terms = [
+        remote(rt.at[peers[k][2]], rr.at[k], es.at[k], er.at[k], peers[k])
+        for k in range(ep_count - 1)
+    ]
+    for copy in terms:
+        copy.start()
+
+    relay_sum(0)
+    relay_sum(1)
+    for m in grad_order:
         gradient(m, f)
+
+    servings = [remote(sv.at[m], other.at[m], svs.at[m], svr.at[m], p_id) for m in range(3)]
+
+    def finish(i):
+        m = grad_order[i]
+        spot = pl.ds((i % 2) * half_cols, half_cols)
+        for copy in load(i):
+            copy.wait()
+        for copy in lasts[m]:
+            copy.wait_recv()
+
+        @pl.loop(0, dep // block)
+        def _(b):
+            rows = pl.ds(pl.multiple_of(b * block, block), block)
+            grad = (
+                sg[m, f, rows, :].astype(jnp.float32)
+                + px[m, rows, :].astype(jnp.float32)
+                + py[m, rows, :].astype(jnp.float32)
+            )
+            grad_out[m, rows, :] = grad
+            after = adam(grad, gate[rows, spot], up[rows, spot], gh[rows, spot])[0]
+            sv[m, rows, :] = after.astype(jnp.bfloat16)
+
+        servings[m].start()
+
+    finish(0)
+    for copy in load(2):
+        copy.start()
+    finish(1)
     for k in range(ep_count - 1):
         terms[k].wait_recv()
     total = rt[e].astype(jnp.float32)
     for k in range(ep_count - 1):
         total = total + rr[k].astype(jnp.float32)
     lo_out[...] = total.astype(jnp.bfloat16)
-
-    for m in range(3):
-        for copy in lasts[m]:
-            copy.wait_recv()
-        grad_out[m] = (
-            sg[m, f].astype(jnp.float32) + px[m].astype(jnp.float32) + py[m].astype(jnp.float32)
-        )
+    finish(2)
+    for copy in servings:
+        copy.wait()
 
     for m in order:
         for copy in (*directs[m], *forwards[m], *shares[m], *firsts[m], *lasts[m]):
@@ -327,6 +394,26 @@
     def _():
         for copy in to_rollout:
             copy.wait_send()
+
+
+def state_kernel(grad, master, moment_one, moment_two, other, master_out, one_out, two_out, serve_out):
+    g = lax.axis_index("group")
+    half = grad.shape[2]
+    after, one, two = adam(grad[...], master[...], moment_one[...], moment_two[...])
+    master_out[...] = after
+    one_out[...] = one
+    two_out[...] = two
+    own = after.astype(jnp.bfloat16)
+
+    @pl.when(g == 0)
+    def _():
+        serve_out[:, :, :half] = own
+        serve_out[:, :, half:] = other[...]
+
+    @pl.when(g == 1)
+    def _():
+        serve_out[:, :, :half] = other[...]
+        serve_out[:, :, half:] = own
 
 
 def kernel_local(
@@ -340,19 +427,21 @@
     ep_count = lax.axis_size("ep")
     parts = lax.axis_size("fsdp")
     tokens_total = steps * row_count * parts
-    ids = jnp.transpose(expert_ids[0], (2, 0, 1))
-    probs = jnp.transpose(route_weights[0], (2, 0, 1))
+    ids = jnp.transpose(expert_ids[0], (0, 2, 1))
+    probs = jnp.transpose(route_weights[0], (0, 2, 1))
     vmem = pl.BlockSpec(memory_space=pltpu.VMEM)
     half_b, f32 = jnp.bfloat16, jnp.float32
     dma = pltpu.SemaphoreType.DMA
-    layer_out, grad_own = pl.pallas_call(
+    anywhere = pl.BlockSpec(memory_space=pl.ANY)
+    layer_out, grad_own, other = pl.pallas_call(
         functools.partial(layer_kernel, ep_count, tokens_total),
         out_shape=(
             jax.ShapeDtypeStruct((steps, row_count // ep_count, feat), half_b),
             jax.ShapeDtypeStruct((3, dep, half), f32),
+            jax.ShapeDtypeStruct((3, dep, half), half_b),
         ),
-        in_specs=[vmem] * 4 + [pl.BlockSpec(memory_space=pl.ANY)],
-        out_specs=(vmem, vmem),
+        in_specs=[vmem] * 4 + [anywhere] * 4,
+        out_specs=(vmem, vmem, vmem),
         scratch_shapes=[
             pltpu.VMEM((3, parts, dep, hidden_count), half_b),
             pltpu.VMEM((slots, hidden_count), f32),
@@ -374,22 +463,36 @@
             pltpu.VMEM((3, dep, half), half_b),
             pltpu.VMEM((ep_count, steps, row_count // ep_count, feat), half_b),
             pltpu.VMEM((ep_count - 1, steps, row_count // ep_count, feat), half_b),
+            pltpu.VMEM((3, dep, half), half_b),
         ]
         + [dma((3,))] * 9
         + [dma((3, 3))] * 2
         + [dma((5,))] * 2
         + [dma((3, 2))] * 2
         + [dma((3, 4))] * 2
-        + [dma((ep_count - 1,))] * 2,
+        + [dma((ep_count - 1,))] * 2
+        + [dma((3, 3))]
+        + [dma((3,))] * 2,
         compiler_params=pltpu.CompilerParams(
             collective_id=0, has_side_effects=True, vmem_limit_bytes=62 * 1024 * 1024
         ),
-    )(ids, probs, batch[0], cotangent, weights[0])
-    master_next, moment_one_next, moment_two_next = adam(
-        grad_own[None], master, moment_one, moment_two
-    )
-    serving = lax.all_gather(master_next.astype(jnp.bfloat16), "group", axis=3, tiled=True)
-    return (layer_out[None], master_next, moment_one_next, moment_two_next, serving)
+    )(ids, probs, batch[0], cotangent, weights[0], master[0], moment_one[0], moment_two[0])
+    cut = dep // 4
+    narrow = pl.BlockSpec((1, cut, half), lambda m, r: (m, r, 0))
+    wide = pl.BlockSpec((1, cut, hidden_count), lambda m, r: (m, r, 0))
+    state = jax.ShapeDtypeStruct((3, dep, half), f32)
+    master_next, moment_one_next, moment_two_next, serving = pl.pallas_call(
+        state_kernel,
+        grid=(3, dep // cut),
+        out_shape=(state, state, state, jax.ShapeDtypeStruct((3, dep, hidden_count), half_b)),
+        in_specs=[narrow] * 5,
+        out_specs=(narrow, narrow, narrow, wide),
+        compiler_params=pltpu.CompilerParams(vmem_limit_bytes=32 * 1024 * 1024),
+    )(grad_own, master[0], moment_one[0], moment_two[0], other)
+    return tuple(
+        part[None]
+        for part in (layer_out, master_next, moment_one_next, moment_two_next, serving)
+    )
 
 
 def local(batch, expert_ids, route_weights, weights, cotangent, master, moment_one, moment_two):

time: 174 us -> 149 us (0.86)
  waiting for transfers between devices: 13.5 us -> 0 us
  between operations: 14 us -> 0.65 us
  other arithmetic: 8.86 us -> 0 us
  Pallas kernels: 130 us -> 138 us
  local copies, waits for them, and re-layouts: 7.36 us -> 10.2 us
    all_gather x1 -> x0, waiting for transfers between devices: 13.5 us -> none  [kernel_local(): lax.all_gather(master_next.astype(jnp.bfloat16), 'group', axis=3, tiled=T...]
    convert_element_type x1 -> x0, other arithmetic: 8.86 us -> none  [kernel_local(): master_next.astype(jnp.bfloat16)]
    pallas_call x0 -> x1, Pallas kernels: none -> 7.96 us  [kernel_local(): pl.pallas_call(state_kernel, grid=(3, dep // cut), out_shape=(state, stat...]
    unnamed x6 -> x13, local copies, waits for them, and re-layouts: 7.36 us -> 10.2 us
  transfers between devices with their start and end apart: 1 -> 0, of which waited for: 1 -> 0; matrix products, arithmetic and copies ran while one was open for 0% -> 0% of each run, Pallas kernels for 0% -> 0%
where the time goes in v2:
time: 149 us
  Pallas kernels  138 us (93%)
  local copies, waits for them, and re-layouts  10.2 us (7%)
    pallas_call x1, Pallas kernels, kernel_local(): pl.pallas_call(functools.partial(layer_kernel, ep_count, tokens_total), o...  130 us
    unnamed x13, local copies, waits for them, and re-layouts  10.2 us
    pallas_call x1, Pallas kernels, kernel_local(): pl.pallas_call(state_kernel, grid=(3, dep // cut), out_shape=(state, stat...  7.96 us

profile of v2, /device:TPU:0, one launch (start us, length us, event | category | flops | bytes accessed | tf_op | source)
XLA Modules:
  0.0 148.9 jit_solution(12745394828013745244)
XLA Ops:
  0.6 130.1 %shard_map.119 = (bf16[4,32,1536]{2,1,0:T(8,128)(2,1)}, f32[3,384,768]{2,1,0:T(8,128)}, bf16[3,384,768]{2,1,0:T(8,128)(2,1)}) custom-call(s32[4,4,128]{2,1,0:T(4,128)} %bitcast.25, f32[4,4,128]{2,1,0:T(4,128)} %bitcast.26, bf16[4,128,1536]{2,1,0:T(8,128)(2,1)} %bitcast.23, bf16[4,128,1536]{2,1,0:T(8,128)(2,1)} %ct.1, bf16[3,384,1536]{2,1,0:T(8,128)(2,1)} %bitcast.22, ...), custom_call_target="tpu_custom_call" | custom-call | tf_op jit(solution)/shard_map/pallas_call | solution.py:436
  130.7 0.0 copy-start
  130.8 2.0 %copy-done = f32[1,3,384,768]{3,2,1,0:T(8,128)S(1)} copy-done((f32[1,3,384,768]{3,2,1,0:T(8,128)S(1)}, f32[1,3,384,768]{3,2,1,0:T(8,128)}, u32[]{:S(2)}) %copy-start) | copy-done | bytes 3538968
  132.7 0.0 copy-start.1
  132.8 2.0 %copy-done.1 = f32[1,3,384,768]{3,2,1,0:T(8,128)S(1)} copy-done((f32[1,3,384,768]{3,2,1,0:T(8,128)S(1)}, f32[1,3,384,768]{3,2,1,0:T(8,128)}, u32[]{:S(2)}) %copy-start.1) | copy-done | bytes 3538968
  134.8 0.0 copy-start.2
  134.8 2.0 %copy-done.2 = f32[1,3,384,768]{3,2,1,0:T(8,128)S(1)} copy-done((f32[1,3,384,768]{3,2,1,0:T(8,128)S(1)}, f32[1,3,384,768]{3,2,1,0:T(8,128)}, u32[]{:S(2)}) %copy-start.2) | copy-done | bytes 3538968
  136.8 0.0 copy-start.3
  136.8 2.0 %copy-done.3 = f32[3,384,768]{2,1,0:T(8,128)S(1)} copy-done((f32[3,384,768]{2,1,0:T(8,128)S(1)}, f32[3,384,768]{2,1,0:T(8,128)}, u32[]{:S(2)}) %copy-start.3) | copy-done | bytes 3538968
  138.8 0.0 copy-start.4
  138.8 1.5 copy-done.4
  140.2 0.0 copy-start.5
  140.2 8.0 %shard_map.120 = (f32[3,384,768]{2,1,0:T(8,128)}, f32[3,384,768]{2,1,0:T(8,128)}, f32[3,384,768]{2,1,0:T(8,128)}, bf16[3,384,1536]{2,1,0:T(8,128)(2,1)}) custom-call(f32[3,384,768]{2,1,0:T(8,128)S(1)} %copy-done.3, f32[3,384,768]{2,1,0:T(8,128)S(1)} %bitcast.17, f32[3,384,768]{2,1,0:T(8,128)S(1)} %bitcast.19, f32[3,384,768]{2,1,0:T(8,128)S(1)} %bitcast.21, ...), custom_call_target="tpu_custom_call" | custom-call | tf_op jit(solution)/shard_map/pallas_call | solution.py:484
  148.2 0.0 copy-done.5
  148.2 0.7 copy.14
Async XLA Ops:
  130.7 2.0 %copy-start = (f32[1,3,384,768]{3,2,1,0:T(8,128)S(1)}, f32[1,3,384,768]{3,2,1,0:T(8,128)}, u32[]{:S(2)}) copy-start(f32[1,3,384,768]{3,2,1,0:T(8,128)} %param.13) | copy-start | bytes 10616836
  132.7 2.0 %copy-start.1 = (f32[1,3,384,768]{3,2,1,0:T(8,128)S(1)}, f32[1,3,384,768]{3,2,1,0:T(8,128)}, u32[]{:S(2)}) copy-start(f32[1,3,384,768]{3,2,1,0:T(8,128)} %param.14) | copy-start | bytes 10616836
  134.8 2.0 %copy-start.2 = (f32[1,3,384,768]{3,2,1,0:T(8,128)S(1)}, f32[1,3,384,768]{3,2,1,0:T(8,128)}, u32[]{:S(2)}) copy-start(f32[1,3,384,768]{3,2,1,0:T(8,128)} %param.15) | copy-start | bytes 10616836
  136.8 2.0 %copy-start.3 = (f32[3,384,768]{2,1,0:T(8,128)S(1)}, f32[3,384,768]{2,1,0:T(8,128)}, u32[]{:S(2)}) copy-start(f32[3,384,768]{2,1,0:T(8,128)} %get-tuple-element.13.grad) | copy-start | bytes 10616836
  138.8 1.5 copy-start.4
  140.2 8.0 %copy-start.5 = (bf16[4,32,1536]{2,1,0:T(8,128)(2,1)S(1)}, bf16[4,32,1536]{2,1,0:T(8,128)(2,1)}, u32[]{:S(2)}) copy-start(bf16[4,32,1536]{2,1,0:T(8,128)(2,1)} %get-tuple-element.12) | copy-start | bytes 1179652

commit v3 on v2

--- a/solution.py
+++ b/solution.py
@@ -218,14 +218,16 @@
 
     lasts = {m: [to_owner(m, i) for i in range(4)] for m in range(3)}
 
-    def open_sum(m):
-        gradient(m, dn)
-        for copy in firsts[m]:
-            copy.start()
-        gradient(m, xn)
-        lasts[m][0].start()
-        gradient(m, yn)
-        lasts[m][3].start()
+    def open_sum(*matrices):
+        for m in matrices:
+            gradient(m, dn)
+            for copy in firsts[m]:
+                copy.start()
+        for m in matrices:
+            gradient(m, xn)
+            lasts[m][0].start()
+            gradient(m, yn)
+            lasts[m][3].start()
 
     def relay_sum(m):
         firsts[m][1].wait_recv()
@@ -313,8 +315,7 @@
         for i in (2, 3):
             to_rollout[i].wait_recv()
 
-    open_sum(0)
-    open_sum(1)
+    open_sum(0, 1)
 
     share_rows = row_count // ep_count
 
@@ -399,21 +400,30 @@
 def state_kernel(grad, master, moment_one, moment_two, other, master_out, one_out, two_out, serve_out):
     g = lax.axis_index("group")
     half = grad.shape[2]
-    after, one, two = adam(grad[...], master[...], moment_one[...], moment_two[...])
-    master_out[...] = after
-    one_out[...] = one
-    two_out[...] = two
-    own = after.astype(jnp.bfloat16)
+    block = 16
+
+    def write(own_cols, other_cols):
+        @pl.loop(0, grad.shape[1] // block)
+        def _(b):
+            rows = pl.ds(pl.multiple_of(b * block, block), block)
+            after, one, two = adam(
+                grad[0, rows, :], master[0, rows, :], moment_one[0, rows, :], moment_two[0, rows, :]
+            )
+            master_out[0, rows, :] = after
+            one_out[0, rows, :] = one
+            two_out[0, rows, :] = two
+            serve_out[0, rows, own_cols] = after.astype(jnp.bfloat16)
+            serve_out[0, rows, other_cols] = other[0, rows, :]
+
+    low, high = pl.ds(0, half), pl.ds(half, half)
 
     @pl.when(g == 0)
     def _():
-        serve_out[:, :, :half] = own
-        serve_out[:, :, half:] = other[...]
+        write(low, high)
 
     @pl.when(g == 1)
     def _():
-        serve_out[:, :, :half] = other[...]
-        serve_out[:, :, half:] = own
+        write(high, low)
 
 
 def kernel_local(
@@ -477,7 +487,7 @@
             collective_id=0, has_side_effects=True, vmem_limit_bytes=62 * 1024 * 1024
         ),
     )(ids, probs, batch[0], cotangent, weights[0], master[0], moment_one[0], moment_two[0])
-    cut = dep // 4
+    cut = dep // 2
     narrow = pl.BlockSpec((1, cut, half), lambda m, r: (m, r, 0))
     wide = pl.BlockSpec((1, cut, hidden_count), lambda m, r: (m, r, 0))
     state = jax.ShapeDtypeStruct((3, dep, half), f32)
@@ -487,7 +497,7 @@
         out_shape=(state, state, state, jax.ShapeDtypeStruct((3, dep, hidden_count), half_b)),
         in_specs=[narrow] * 5,
         out_specs=(narrow, narrow, narrow, wide),
-        compiler_params=pltpu.CompilerParams(vmem_limit_bytes=32 * 1024 * 1024),
+        compiler_params=pltpu.CompilerParams(vmem_limit_bytes=60 * 1024 * 1024),
     )(grad_own, master[0], moment_one[0], moment_two[0], other)
     return tuple(
         part[None]

time: 149 us -> 144 us (0.966)
  local copies, waits for them, and re-layouts: 10.2 us -> 0.75 us
  Pallas kernels: 138 us -> 143 us
    unnamed x13 -> x3, local copies, waits for them, and re-layouts: 10.2 us -> 0.75 us
    pallas_call x1, Pallas kernels: 7.96 us -> 12.6 us  [kernel_local(): pl.pallas_call(state_kernel, grid=(3, dep // cut), out_shape=(state, stat...]
where the time goes in v3:
time: 144 us
  Pallas kernels  143 us (99%)
    pallas_call x1, Pallas kernels, kernel_local(): pl.pallas_call(functools.partial(layer_kernel, ep_count, tokens_total), o...  130 us
    pallas_call x1, Pallas kernels, kernel_local(): pl.pallas_call(state_kernel, grid=(3, dep // cut), out_shape=(state, stat...  12.6 us

profile of v3, /device:TPU:0, one launch (start us, length us, event | category | flops | bytes accessed | tf_op | source)
XLA Modules:
  0.0 144.1 jit_solution(4799360724947441428)
XLA Ops:
  0.6 130.1 %shard_map.119 = (bf16[4,32,1536]{2,1,0:T(8,128)(2,1)}, f32[3,384,768]{2,1,0:T(8,128)}, bf16[3,384,768]{2,1,0:T(8,128)(2,1)}) custom-call(s32[4,4,128]{2,1,0:T(4,128)} %bitcast.25, f32[4,4,128]{2,1,0:T(4,128)} %bitcast.26, bf16[4,128,1536]{2,1,0:T(8,128)(2,1)} %bitcast.23, bf16[4,128,1536]{2,1,0:T(8,128)(2,1)} %ct.1, bf16[3,384,1536]{2,1,0:T(8,128)(2,1)} %bitcast.22, ...), custom_call_target="tpu_custom_call" | custom-call | tf_op jit(solution)/shard_map/pallas_call | solution.py:446
  130.7 0.0 copy-start
  130.7 12.6 %shard_map.120 = (f32[3,384,768]{2,1,0:T(8,128)}, f32[3,384,768]{2,1,0:T(8,128)}, f32[3,384,768]{2,1,0:T(8,128)}, bf16[3,384,1536]{2,1,0:T(8,128)(2,1)}) custom-call(f32[3,384,768]{2,1,0:T(8,128)} %get-tuple-element.13.grad, f32[3,384,768]{2,1,0:T(8,128)} %bitcast.17, f32[3,384,768]{2,1,0:T(8,128)} %bitcast.19, f32[3,384,768]{2,1,0:T(8,128)} %bitcast.21, ...), custom_call_target="tpu_custom_call" | custom-call | tf_op jit(solution)/shard_map/pallas_call | solution.py:494
  143.4 0.0 copy-done
  143.4 0.7 copy.14
Async XLA Ops:
  130.7 12.7 %copy-start = (bf16[4,32,1536]{2,1,0:T(8,128)(2,1)S(1)}, bf16[4,32,1536]{2,1,0:T(8,128)(2,1)}, u32[]{:S(2)}) copy-start(bf16[4,32,1536]{2,1,0:T(8,128)(2,1)} %get-tuple-element.12) | copy-start | bytes 1179652
